TPU v7x, 32 devices: a whole 2x2x4 slice. The times are simulated.
32 devices in a mesh: dp: 4 (over y, x), latent: 8 (over z, core).
Axes of the slice: x: 2, y: 2, z: 4, core: 2. Of those that a mesh axis runs over, the one named last changes fastest.
Arguments:
- paired: bfloat16 [1024, 8192], P('dp'), may hold values from -6 to 6
- enc_weight: float32 [8192, 8192], P('dp', 'latent'), may hold values from -0.0625 to 0.0625
- enc_bias: float32 [8192], P('latent'), may hold values from -3 to 3
- dec_weight: float32 [8192, 8192], P('latent', 'dp'), may hold values from -0.21931359 to 0.21931359
- dec_bias: float32 [8192], P('dp'), may hold values from -3 to 3
- buffer_rows: bfloat16 [4096, 8192], P('dp', 'latent'), may hold values from -6 to 6
- block_dest: int32 [64], replicated, may hold values from 0 to 63, as said below
Outputs:
- enc_grad: float32 [8192, 8192], P('dp', 'latent')
- dec_grad: float32 [8192, 8192], P('latent', 'dp')
- shuffled: bfloat16 [4096, 8192], P('dp', 'latent')
Inputs may be any that keep to these rules, and one draw needn't show every extreme that they name: `block_dest`: a permutation of the 64 blocks; the 16 blocks of each index of dp go exactly 4 to each index of dp.
All inputs are finite; a program needn't handle non-finite values.
Results may differ from a plain program's by a relative error of at most 0.014.
Values may be sent and summed in bfloat16 or wider, within the bound.
A program may use at most 192 MiB of HBM per device.

v0:
```python
import jax
import jax.numpy as jnp
from jax import lax
from jax.sharding import PartitionSpec as P

BLOCK_ROWS = 64


loss_scale = 0.03125
sparsity_weight = 4.0
norm_eps = 1e-06


def body(paired, enc_weight, enc_bias, dec_weight, dec_bias, buffer_rows, block_dest):
    data_count = lax.axis_size("dp")
    latent_count = lax.axis_size("latent")
    data_index = lax.axis_index("dp")
    latent_index = lax.axis_index("latent")
    own_rows = paired.shape[0]
    total_rows = own_rows * data_count
    error_count = total_rows // latent_count
    enc16 = enc_weight.astype(jnp.bfloat16)
    dec16 = dec_weight.astype(jnp.bfloat16)
    contract_rows = (((0,), (0,)), ((), ()))
    contract_cols = (((1,), (1,)), ((), ()))
    column_rows = lax.all_to_all(paired, "dp", split_axis=1, concat_axis=0, tiled=True)
    feature_block = paired
    preact = jnp.dot(
        feature_block,
        lax.all_gather(enc16, "dp", axis=0, tiled=True),
        preferred_element_type=jnp.float32,
    )
    preact = preact + enc_bias
    activated = jnp.maximum(preact, 0.0)
    latent_codes = (activated * activated).astype(jnp.bfloat16)
    all_codes = lax.all_gather(latent_codes, "dp", axis=0, tiled=True)
    row_block = all_codes
    recon = (
        lax.psum_scatter(
            jnp.dot(row_block, dec16, preferred_element_type=jnp.float32).astype(jnp.bfloat16),
            "latent",
            scatter_dimension=0,
            tiled=True,
        ).astype(jnp.float32)
        + dec_bias
    )
    target_rows = lax.dynamic_slice_in_dim(column_rows, latent_index * error_count, error_count, 0)
    recon_error = recon - target_rows.astype(jnp.float32)
    half_count = data_count // 2
    model_index = data_index // half_count
    local_squares = jnp.sum(dec_weight * dec_weight, axis=1)
    square_pair = jnp.stack(
        [
            jnp.where(model_index == 0, local_squares, 0.0),
            jnp.where(model_index == 1, local_squares, 0.0),
        ]
    )
    square_sums = lax.psum(square_pair, "dp")
    dec_norms = jnp.sqrt(square_sums + norm_eps)
    own_norm = jnp.where(model_index == 0, dec_norms[0], dec_norms[1])
    error_grad = (2.0 * loss_scale * recon_error).astype(jnp.bfloat16)
    all_errors = lax.all_gather(error_grad, "latent", axis=0, tiled=True)
    code_sum = jnp.sum(all_codes, axis=0, dtype=jnp.float32)
    dec_main = lax.dot_general(
        all_codes, all_errors, contract_rows, preferred_element_type=jnp.float32
    )
    dec_grad = (
        dec_main + sparsity_weight * loss_scale * code_sum[:, None] * dec_weight / own_norm[:, None]
    )
    row_block = all_errors
    code_grad = lax.psum_scatter(
        lax.dot_general(row_block, dec16, contract_cols, preferred_element_type=jnp.float32).astype(
            jnp.bfloat16
        ),
        "dp",
        scatter_dimension=0,
        tiled=True,
    ).astype(jnp.float32)
    code_grad = code_grad + sparsity_weight * loss_scale * (dec_norms[0] + dec_norms[1])
    preact_grad = (code_grad * 2.0 * activated).astype(jnp.bfloat16)
    feature_block = paired
    enc_grad = lax.psum_scatter(
        lax.dot_general(
            feature_block, preact_grad, contract_rows, preferred_element_type=jnp.float32
        ).astype(jnp.bfloat16),
        "dp",
        scatter_dimension=0,
        tiled=True,
    ).astype(jnp.float32)
    blocks_here = buffer_rows.shape[0] // BLOCK_ROWS
    per_device = blocks_here // data_count
    block_iota = jnp.arange(blocks_here, dtype=jnp.int32)
    own_dest = lax.dynamic_slice_in_dim(block_dest, data_index * blocks_here, blocks_here, 0)
    target_device = own_dest // blocks_here
    earlier_same = (target_device[None, :] == target_device[:, None]) & (
        own_dest[None, :] < own_dest[:, None]
    )
    send_slot = target_device * per_device + jnp.sum(earlier_same.astype(jnp.int32), axis=1)
    chosen = jnp.sum(
        jnp.where(send_slot[None, :] == block_iota[:, None], block_iota[None, :], 0), axis=1
    )
    feature_count = buffer_rows.shape[1]
    outgoing = buffer_rows.reshape(blocks_here, BLOCK_ROWS, feature_count)[chosen].reshape(
        buffer_rows.shape
    )
    arrived = lax.all_to_all(outgoing, "dp", split_axis=0, concat_axis=0, tiled=True)
    positions = data_index * blocks_here + block_iota
    every_block = jnp.arange(block_dest.shape[0], dtype=jnp.int32)
    source_block = jnp.sum(
        jnp.where(block_dest[None, :] == positions[:, None], every_block[None, :], 0), axis=1
    )
    sender_device = source_block // blocks_here
    before_same = (sender_device[None, :] == sender_device[:, None]) & (
        block_iota[None, :] < block_iota[:, None]
    )
    arrival_slot = sender_device * per_device + jnp.sum(before_same.astype(jnp.int32), axis=1)
    shuffled = arrived.reshape(blocks_here, BLOCK_ROWS, feature_count)[arrival_slot].reshape(
        buffer_rows.shape
    )
    return (enc_grad, dec_grad, shuffled)


def solution(mesh):
    in_specs = (
        P("dp", None),
        P("dp", "latent"),
        P("latent"),
        P("latent", "dp"),
        P("dp"),
        P("dp", "latent"),
        P(),
    )
    out_specs = (P("dp", "latent"), P("latent", "dp"), P("dp", "latent"))
    return jax.shard_map(body, mesh=mesh, in_specs=in_specs, out_specs=out_specs, check_vma=False)
```

profile of v0, /device:TPU:0, one launch (start us, length us, event | category | flops | bytes accessed | tf_op | source)
XLA Modules:
  0.0 586.9 jit_solution(17896344670219617063)
XLA Ops:
  7.2 6.2 %convert_element_type.48 = bf16[2048,1024]{1,0:T(8,128)(2,1)} convert(f32[2048,1024]{1,0:T(8,128)} %param.8) | non-fusion elementwise | flops 2097152 | bytes 12582912 | tf_op jit(solution)/shard_map/convert_element_type | solution.py:22
  13.5 0.0 all-gather.6.cloned.1.call-start
  13.5 160.2 %all-gather.4.cloned.1.call-done = bf16[8192,1024]{1,0:T(8,128)(2,1)} async-done(((bf16[2048,1024]{1,0:T(8,128)(2,1)}), bf16[8192,1024]{1,0:T(8,128)(2,1)}) %all-gather.4.cloned.1.call-update) | async-done | bytes 16777232 | tf_op jit(solution)/shard_map/all_gather | solution.py:30
  173.7 12.3 %multiply_convert_fusion.2 = (bf16[256,1024]{1,0:T(8,128)(2,1)}, f32[256,1024]{1,0:T(8,128)S(1)}) fusion(f32[1024]{0:T(1024)S(1)} %copy-done.3, bf16[256,8192]{1,0:T(8,128)(2,1)} %param.7, bf16[8192,1024]{1,0:T(8,128)(2,1)} %all-gather.4.cloned.1.call-done), kind=kOutput, calls=%fused_computation.16 | convolution fusion | flops 4296015872 | bytes 22548480 | tf_op jit(solution)/shard_map/dot_general | solution.py:28
  186.1 35.4 %all-gather.6.cloned.1.call-done = bf16[1024,1024]{1,0:T(8,128)(2,1)} async-done(((bf16[256,1024]{1,0:T(8,128)(2,1)}), bf16[1024,1024]{1,0:T(8,128)(2,1)}) %all-gather.6.cloned.1.call-update) | async-done | bytes 2097168 | tf_op jit(solution)/shard_map/all_gather | solution.py:36
  221.6 10.5 %convolution_convert_fusion = bf16[1024,2048]{1,0:T(8,128)(2,1)} fusion(bf16[1024,1024]{1,0:T(8,128)(2,1)} %all-gather.6.cloned.1.call-done, f32[1024,2048]{1,0:T(8,128)} %param.10), kind=kOutput, calls=%fused_computation.7 | convolution fusion | flops 4299161600 | bytes 14680064 | tf_op jit(solution)/shard_map/dot_general | solution.py:40
  232.1 4.8 copy.16
  236.9 5.0 all-to-all-start
  241.9 0.0 all-gather.8.cloned.1.call-start
  242.0 47.6 %all-to-all-done = bf16[256,4,2048]{2,0,1:T(8,128)(2,1)} async-done(((bf16[256,4,2048]{2,0,1:T(8,128)(2,1)}), bf16[256,4,2048]{2,0,1:T(8,128)(2,1)}, u32[]{:S(2)}, u32[]{:S(2)}) %all-to-all-start) | async-done | bytes 4194336 | tf_op jit(solution)/shard_map/all_to_all | solution.py:26
  289.6 2.2 multiply_convert_fusion.1
  291.8 0.2 reduce-scatter.6.cloned.1.call-start
  292.1 47.1 %all-gather.8.cloned.1.call-done = bf16[1024,2048]{1,0:T(8,128)(2,1)} async-done(((bf16[128,2048]{1,0:T(8,128)(2,1)}), bf16[1024,2048]{1,0:T(8,128)(2,1)}) %all-gather.8.cloned.1.call-update) | async-done | bytes 4194320 | tf_op jit(solution)/shard_map/all_gather | solution.py:62
  339.1 10.5 %fusion.3 = bf16[1024,1024]{1,0:T(8,128)(2,1)} fusion(bf16[1024,2048]{1,0:T(8,128)(2,1)} %all-gather.8.cloned.1.call-done, f32[1024,2048]{1,0:T(8,128)} %param.10), kind=kOutput, calls=%fused_computation.11 | convolution fusion | flops 4298113024 | bytes 14680064 | tf_op jit(solution)/shard_map/dot_general | solution.py:72
  349.7 4.0 multiply_reduce_fusion
  353.8 10.5 %psum.7 = f32[2,1024]{1,0:T(2,128)S(1)} all-reduce(f32[2,1024]{1,0:T(2,128)S(1)} %pad_maximum_fusion), channel_id=1, replica_groups=mesh['dp'=4,'latent'=8] {'dp'}, use_global_device_ids=true, to_apply=%region_3.4 | all-reduce | flops 2048 | bytes 16384 | tf_op jit(solution)/shard_map/psum | solution.py:58
  364.3 19.8 %reduce-scatter.6.cloned.1.call-done = bf16[256,1024]{1,0:T(8,128)(2,1)} async-done(((bf16[1024,1024]{1,0:T(8,128)(2,1)}), bf16[256,1024]{1,0:T(8,128)(2,1)}) %reduce-scatter.6.cloned.1.call-update) | async-done | bytes 524304 | tf_op jit(solution)/shard_map/reduce_scatter | solution.py:71
  384.0 12.7 %convert_bitcast_fusion = bf16[8192,1024]{0,1:T(8,128)(2,1)} fusion(bf16[256,8192]{1,0:T(8,128)(2,1)} %param.7, f32[256,1024]{1,0:T(8,128)S(1)} %get-tuple-element.16, bf16[256,1024]{1,0:T(8,128)(2,1)} %reduce-scatter.6.cloned.1.call-done, f32[1024]{0:T(1024)S(1)} %bitcast.49), kind=kOutput, calls=%fused_computation.2 | convolution fusion | flops 4304666624 | bytes 22548480 | tf_op jit(solution)/shard_map/dot_general | solution.py:83
  396.7 0.6 copy-done.2
  397.4 0.1 and_select_fusion.2
  397.5 0.2 convert_reduce_fusion.2
  397.6 0.1 select_reduce_fusion.1
  397.8 2.0 gather_fusion
  399.8 4.7 all-to-all-start.1
  404.5 0.2 select_reduce_fusion
  404.7 0.2 convert_reduce_fusion.1
  404.9 47.7 %all-to-all-done.1 = bf16[4,256,1024]{2,1,0:T(8,128)(2,1)} async-done(((bf16[4,256,1024]{2,1,0:T(8,128)(2,1)}), bf16[4,256,1024]{2,1,0:T(8,128)(2,1)}, u32[]{:S(2)}, u32[]{:S(2)}) %all-to-all-start.1) | async-done | bytes 2097184 | tf_op jit(solution)/shard_map/all_to_all | solution.py:106
  452.6 3.6 gather_fusion.1
  456.2 2.0 convert_reduce_fusion
  458.1 13.7 %divide_add_fusion = f32[1024,2048]{1,0:T(8,128)} fusion(f32[1024,2048]{1,0:T(8,128)} %param.10, f32[1024]{0:T(1024)S(1)} %bitcast.52, f32[1024]{0:T(1024)S(1)} %broadcast_multiply_fusion, bf16[1024,1024]{1,0:T(8,128)(2,1)} %all-gather.6.cloned.1.call-done, bf16[1024,2048]{1,0:T(8,128)(2,1)} %all-gather.8.cloned.1.call-done), kind=kOutput, calls=%fused_computation.3 | convolution fusion | flops 4301258752 | bytes 23076864 | tf_op jit(solution)/shard_map/dot_general | solution.py:64
  471.9 101.3 %reduce-scatter.8.cloned.1.call-done = bf16[2048,1024]{0,1:T(8,128)(2,1)} async-done(((bf16[8192,1024]{0,1:T(8,128)(2,1)}), bf16[2048,1024]{0,1:T(8,128)(2,1)}) %reduce-scatter.8.cloned.1.call-update) | async-done | bytes 4194320 | tf_op jit(solution)/shard_map/reduce_scatter | solution.py:82
  573.2 6.9 %copy.13 = f32[2048,1024]{1,0:T(8,128)} copy(bf16[2048,1024]{0,1:T(8,128)(2,1)} %reduce-scatter.8.cloned.1.call-done) | data formatting | bytes 12582912
  (29 shorter events, 0.3 us)
Async XLA Ops:
  7.2 390.6 %copy-start = (bf16[1024,1024]{1,0:T(8,128)(2,1)S(1)}, bf16[1024,1024]{1,0:T(8,128)(2,1)}, u32[]{:S(2)}) copy-start(bf16[1024,1024]{1,0:T(8,128)(2,1)} %param.12) | copy-start | bytes 6291460
  7.2 166.6 %all-gather.4.cloned.1.call-start = ((), (), s32[]{:S(2)}) async-start(), calls=%async_computation.5 | async-start | bytes 20971520 | tf_op jit(solution)/shard_map/all_gather | solution.py:30
  13.4 160.3 %copy-start.3 = (f32[1024]{0:T(1024)S(1)}, f32[1024]{0:T(1024)}, u32[]{:S(2)}) copy-start(f32[1024]{0:T(1024)} %param.9) | copy-start | bytes 12292
  13.5 208.1 %all-gather.6.cloned.1.call-start = ((), (), s32[]{:S(2)}) async-start(), calls=%async_computation.6 | async-start | bytes 2621440 | tf_op jit(solution)/shard_map/all_gather | solution.py:36
  186.1 103.5 %reduce-scatter.4.cloned.1.call-start = ((), (), s32[]{:S(2)}) async-start(), calls=%async_computation.7 | async-start | bytes 4718592 | tf_op jit(solution)/shard_map/reduce_scatter | solution.py:39
  236.9 52.7 %copy-start.1 = (f32[2048]{0:T(1024)S(1)}, f32[2048]{0:T(1024)}, u32[]{:S(2)}) copy-start(f32[2048]{0:T(1024)} %param.11) | copy-start | bytes 24580
  236.9 52.7 %all-to-all-start = ((bf16[256,4,2048]{2,0,1:T(8,128)(2,1)}), bf16[256,4,2048]{2,0,1:T(8,128)(2,1)}, u32[]{:S(2)}, u32[]{:S(2)}) async-start(bf16[256,4,2048]{2,0,1:T(8,128)(2,1)} %bitcast.46), calls=%async_computation.1 | async-start | bytes 8388608 | tf_op jit(solution)/shard_map/all_to_all | solution.py:26
  241.9 97.2 %all-gather.8.cloned.1.call-start = ((), (), s32[]{:S(2)}) async-start(), calls=%async_computation.8 | async-start | bytes 4718592 | tf_op jit(solution)/shard_map/all_gather | solution.py:62
  291.8 92.2 %reduce-scatter.6.cloned.1.call-start = ((), (), s32[]{:S(2)}) async-start(), calls=%async_computation.9 | async-start | bytes 2621440 | tf_op jit(solution)/shard_map/reduce_scatter | solution.py:71
  349.7 223.6 %reduce-scatter.8.cloned.1.call-start = ((), (), s32[]{:S(2)}) async-start(), calls=%async_computation.10 | async-start | bytes 20971520 | tf_op jit(solution)/shard_map/reduce_scatter | solution.py:82
  396.7 0.7 copy-start.2
  399.8 52.8 %all-to-all-start.1 = ((bf16[4,256,1024]{2,1,0:T(8,128)(2,1)}), bf16[4,256,1024]{2,1,0:T(8,128)(2,1)}, u32[]{:S(2)}, u32[]{:S(2)}) async-start(bf16[4,256,1024]{2,1,0:T(8,128)(2,1)} %bitcast.47), calls=%async_computation.4 | async-start | bytes 4194304 | tf_op jit(solution)/shard_map/all_to_all | solution.py:106
Sparse Core Ops, SparseCore 0:
  13.6 160.1 all-gather.3
  186.2 35.3 all-gather.5
  232.2 49.9 reduce-scatter.3
  292.0 47.1 all-gather.7
  349.8 34.2 reduce-scatter.5
  396.9 176.3 reduce-scatter.7
where the time goes:
time: 588 us; the launch traced here: 587 us
  waiting for transfers between devices  459 us (78%)
  matrix products  59.8 us (10%)
  local copies, waits for them, and re-layouts  17.9 us (3%)
  other arithmetic  15.2 us (3%)
  between operations  14.2 us (2%)
  blocking collectives  10.5 us (2%)
  starting transfers between devices  10.1 us (2%)
    all_gather x1, waiting for transfers between devices, body(): lax.all_gather(enc16, 'dp', axis=0, tiled=True)  160 us
    reduce_scatter x1, waiting for transfers between devices, body(): lax.psum_scatter(lax.dot_general(feature_block, preact_grad, contract_row...  101 us
    all_to_all x1, waiting for transfers between devices, body(): lax.all_to_all(outgoing, 'dp', split_axis=0, concat_axis=0, tiled=True)  47.7 us
    all_to_all x1, waiting for transfers between devices, body(): lax.all_to_all(paired, 'dp', split_axis=1, concat_axis=0, tiled=True)  47.6 us
    all_gather x1, waiting for transfers between devices, body(): all_errors = lax.all_gather(error_grad, 'latent', axis=0, tiled=True)  47.1 us
    all_gather x1, waiting for transfers between devices, body(): all_codes = lax.all_gather(latent_codes, 'dp', axis=0, tiled=True)  35.4 us
    reduce_scatter x1, waiting for transfers between devices, body(): lax.psum_scatter(lax.dot_general(row_block, dec16, contract_cols, preferr...  19.8 us
    dot_general x1, matrix products, body(): lax.dot_general(all_codes, all_errors, contract_rows, preferred_element_t...  13.7 us
  transfers between devices with their start and end apart: 8, of which 7 were waited for; matrix products, arithmetic and copies ran while one was open for 5% of the time, Pallas kernels for 0%

commit v1 on v0

--- a/solution.py
+++ b/solution.py
@@ -24,12 +24,12 @@
     contract_rows = (((0,), (0,)), ((), ()))
     contract_cols = (((1,), (1,)), ((), ()))
     column_rows = lax.all_to_all(paired, "dp", split_axis=1, concat_axis=0, tiled=True)
-    feature_block = paired
-    preact = jnp.dot(
-        feature_block,
-        lax.all_gather(enc16, "dp", axis=0, tiled=True),
-        preferred_element_type=jnp.float32,
-    )
+    preact = lax.psum_scatter(
+        jnp.dot(column_rows, enc16, preferred_element_type=jnp.float32).astype(jnp.bfloat16),
+        "dp",
+        scatter_dimension=0,
+        tiled=True,
+    ).astype(jnp.float32)
     preact = preact + enc_bias
     activated = jnp.maximum(preact, 0.0)
     latent_codes = (activated * activated).astype(jnp.bfloat16)
@@ -78,15 +78,10 @@
     ).astype(jnp.float32)
     code_grad = code_grad + sparsity_weight * loss_scale * (dec_norms[0] + dec_norms[1])
     preact_grad = (code_grad * 2.0 * activated).astype(jnp.bfloat16)
-    feature_block = paired
-    enc_grad = lax.psum_scatter(
-        lax.dot_general(
-            feature_block, preact_grad, contract_rows, preferred_element_type=jnp.float32
-        ).astype(jnp.bfloat16),
-        "dp",
-        scatter_dimension=0,
-        tiled=True,
-    ).astype(jnp.float32)
+    all_preact_grads = lax.all_gather(preact_grad, "dp", axis=0, tiled=True)
+    enc_grad = lax.dot_general(
+        column_rows, all_preact_grads, contract_rows, preferred_element_type=jnp.float32
+    )
     blocks_here = buffer_rows.shape[0] // BLOCK_ROWS
     per_device = blocks_here // data_count
     block_iota = jnp.arange(blocks_here, dtype=jnp.int32)

time: 588 us -> 384 us (0.65)
  waiting for transfers between devices: 459 us -> 195 us
  blocking collectives: 10.5 us -> 87.5 us
  matrix products: 59.8 us -> 51.2 us
  starting transfers between devices: 10.1 us -> 3.89 us
    all_gather x1, waiting for transfers between devices: 160 us -> 17.1 us  [body(): all_preact_grads = lax.all_gather(preact_grad, 'dp', axis=0, tiled=True)]
    reduce_scatter x1, waiting for transfers between devices: 101 us -> 35 us  [body(): lax.psum_scatter(jnp.dot(column_rows, enc16, preferred_element_type=jnp.f...]
    all_to_all x0 -> x1, blocking collectives: none -> 53.1 us  [body(): lax.all_to_all(paired, 'dp', split_axis=1, concat_axis=0, tiled=True)]
    reduce_scatter x1, waiting for transfers between devices: 0.01 us -> 50.1 us  [body(): lax.psum_scatter(jnp.dot(row_block, dec16, preferred_element_type=jnp.flo...]
    all_to_all x1, waiting for transfers between devices: 47.7 us -> 0.01 us  [body(): lax.all_to_all(outgoing, 'dp', split_axis=0, concat_axis=0, tiled=True)]
    all_to_all x1 -> x0, waiting for transfers between devices: 47.6 us -> none  [body(): lax.all_to_all(paired, 'dp', split_axis=1, concat_axis=0, tiled=True)]
    psum x1, blocking collectives: 10.5 us -> 34.4 us  [body(): square_sums = lax.psum(square_pair, 'dp')]
    dot_general x2, matrix products: 25 us -> 16.3 us  [the longest x1 10.6 us: body(): lax.dot_general(column_rows, all_preact_grads, contract_rows, preferred_e...]
  transfers between devices with their start and end apart: 8 -> 7, of which waited for: 7 -> 6; matrix products, arithmetic and copies ran while one was open for 5% -> 7% of each run, Pallas kernels for 0% -> 0%
where the time goes in v1:
time: 384 us; the launch traced here: 383 us
  waiting for transfers between devices  195 us (51%)
  blocking collectives  87.5 us (23%)
  matrix products  51.2 us (13%)
  local copies, waits for them, and re-layouts  18.1 us (5%)
  between operations  14.3 us (4%)
  other arithmetic  13.2 us (3%)
  starting transfers between devices  3.89 us (1%)
    all_to_all x1, blocking collectives, body(): lax.all_to_all(paired, 'dp', split_axis=1, concat_axis=0, tiled=True)  53.1 us
    reduce_scatter x1, waiting for transfers between devices, body(): lax.psum_scatter(jnp.dot(row_block, dec16, preferred_element_type=jnp.flo...  50.1 us
    all_gather x1, waiting for transfers between devices, body(): all_errors = lax.all_gather(error_grad, 'latent', axis=0, tiled=True)  45.4 us
    all_gather x1, waiting for transfers between devices, body(): all_codes = lax.all_gather(latent_codes, 'dp', axis=0, tiled=True)  35.8 us
    reduce_scatter x1, waiting for transfers between devices, body(): lax.psum_scatter(jnp.dot(column_rows, enc16, preferred_element_type=jnp.f...  35 us
    psum x1, blocking collectives, body(): square_sums = lax.psum(square_pair, 'dp')  34.4 us
    all_gather x1, waiting for transfers between devices, body(): all_preact_grads = lax.all_gather(preact_grad, 'dp', axis=0, tiled=True)  17.1 us
    dot_general x1, matrix products, body(): lax.dot_general(all_codes, all_errors, contract_rows, preferred_element_t...  13.9 us
  transfers between devices with their start and end apart: 7, of which 6 were waited for; matrix products, arithmetic and copies ran while one was open for 7% of the time, Pallas kernels for 0%

profile of v1, /device:TPU:0, one launch (start us, length us, event | category | flops | bytes accessed | tf_op | source)
XLA Modules:
  0.0 383.1 jit_solution(7814965590232072697)
XLA Ops:
  7.2 2.7 copy.16
  9.9 53.1 %all_to_all.28 = bf16[256,4,2048]{2,0,1:T(8,128)(2,1)S(1)} all-to-all(bf16[256,4,2048]{2,0,1:T(8,128)(2,1)S(1)} %bitcast.45), channel_id=1, replica_groups=mesh['dp'=4,'latent'=8] {'dp'}, dimensions={1} | all-to-all | bytes 8388608 | tf_op jit(solution)/shard_map/all_to_all | solution.py:26
  63.0 2.0 copy-done.2
  65.0 5.7 %fusion.8 = bf16[1024,1024]{1,0:T(8,128)(2,1)} fusion(bf16[1024,2048]{1,0:T(8,128)(2,1)S(1)} %bitcast.48, f32[2048,1024]{1,0:T(8,128)S(1)} %bitcast.58), kind=kOutput, calls=%fused_computation.14 | convolution fusion | flops 4298113024 | bytes 14680064 | tf_op jit(solution)/shard_map/dot_general | solution.py:28
  70.7 0.0 all-gather.4.cloned.1.call-start
  70.8 35.0 %reduce-scatter.4.cloned.1.call-done = bf16[256,1024]{1,0:T(8,128)(2,1)} async-done(((bf16[1024,1024]{1,0:T(8,128)(2,1)}), bf16[256,1024]{1,0:T(8,128)(2,1)}) %reduce-scatter.4.cloned.1.call-update) | async-done | bytes 524304 | tf_op jit(solution)/shard_map/reduce_scatter | solution.py:27
  105.8 2.0 multiply_convert_fusion.2
  107.8 0.0 reduce-scatter.6.cloned.1.call-start
  107.9 35.8 %all-gather.4.cloned.1.call-done = bf16[1024,1024]{1,0:T(8,128)(2,1)} async-done(((bf16[256,1024]{1,0:T(8,128)(2,1)}), bf16[1024,1024]{1,0:T(8,128)(2,1)}) %all-gather.4.cloned.1.call-update) | async-done | bytes 2097168 | tf_op jit(solution)/shard_map/all_gather | solution.py:36
  143.7 10.5 %convolution_convert_fusion = bf16[1024,2048]{1,0:T(8,128)(2,1)} fusion(bf16[1024,1024]{1,0:T(8,128)(2,1)} %all-gather.4.cloned.1.call-done, f32[1024,2048]{1,0:T(8,128)} %param.10), kind=kOutput, calls=%fused_computation.9 | convolution fusion | flops 4299161600 | bytes 14680064 | tf_op jit(solution)/shard_map/dot_general | solution.py:40
  154.2 0.0 all-gather.6.cloned.1.call-start
  154.3 50.1 %reduce-scatter.6.cloned.1.call-done = bf16[128,2048]{1,0:T(8,128)(2,1)} async-done(((bf16[1024,2048]{1,0:T(8,128)(2,1)}), bf16[128,2048]{1,0:T(8,128)(2,1)}) %reduce-scatter.6.cloned.1.call-update) | async-done | bytes 524304 | tf_op jit(solution)/shard_map/reduce_scatter | solution.py:39
  204.4 2.2 multiply_convert_fusion.1
  206.7 45.4 %all-gather.6.cloned.1.call-done = bf16[1024,2048]{1,0:T(8,128)(2,1)} async-done(((bf16[128,2048]{1,0:T(8,128)(2,1)}), bf16[1024,2048]{1,0:T(8,128)(2,1)}) %all-gather.6.cloned.1.call-update) | async-done | bytes 4194320 | tf_op jit(solution)/shard_map/all_gather | solution.py:62
  252.1 10.5 %fusion.5 = bf16[1024,1024]{1,0:T(8,128)(2,1)} fusion(bf16[1024,2048]{1,0:T(8,128)(2,1)} %all-gather.6.cloned.1.call-done, f32[1024,2048]{1,0:T(8,128)} %param.10), kind=kOutput, calls=%fused_computation.13 | convolution fusion | flops 4298113024 | bytes 14680064 | tf_op jit(solution)/shard_map/dot_general | solution.py:72
  262.6 0.1 and_select_fusion.2
  262.7 0.2 convert_reduce_fusion.2
  262.9 0.1 select_reduce_fusion.1
  263.0 2.0 gather_fusion
  265.0 3.6 all-to-all-start.1
  268.7 4.1 %multiply_reduce_fusion = f32[1024]{0:T(1024)S(1)} fusion(f32[1024,2048]{1,0:T(8,128)} %param.10), kind=kLoop, calls=%fused_computation.3 | loop fusion | flops 4193280 | bytes 8392704 | tf_op jit(solution)/shard_map/reduce_sum | solution.py:51
  272.8 34.4 %psum.7 = f32[2,1024]{1,0:T(2,128)S(1)} all-reduce(f32[2,1024]{1,0:T(2,128)S(1)} %pad_maximum_fusion), channel_id=1, replica_groups=mesh['dp'=4,'latent'=8] {'dp'}, use_global_device_ids=true, to_apply=%region_4.5 | all-reduce | flops 2048 | bytes 16384 | tf_op jit(solution)/shard_map/psum | solution.py:58
  307.3 11.4 %reduce-scatter.8.cloned.1.call-done = bf16[256,1024]{1,0:T(8,128)(2,1)} async-done(((bf16[1024,1024]{1,0:T(8,128)(2,1)}), bf16[256,1024]{1,0:T(8,128)(2,1)}) %reduce-scatter.8.cloned.1.call-update) | async-done | bytes 524304 | tf_op jit(solution)/shard_map/reduce_scatter | solution.py:71
  318.7 2.1 multiply_convert_fusion
  320.8 0.2 select_reduce_fusion
  321.0 0.2 convert_reduce_fusion.1
  321.3 2.0 gather_fusion.1
  323.3 2.0 convert_reduce_fusion
  325.2 13.9 %divide_add_fusion = f32[1024,2048]{1,0:T(8,128)} fusion(f32[1024,2048]{1,0:T(8,128)} %param.10, f32[1024]{0:T(1024)S(1)} %bitcast.56, f32[1024]{0:T(1024)S(1)} %broadcast_multiply_fusion, bf16[1024,1024]{1,0:T(8,128)(2,1)} %all-gather.4.cloned.1.call-done, bf16[1024,2048]{1,0:T(8,128)(2,1)} %all-gather.6.cloned.1.call-done), kind=kOutput, calls=%fused_computation.2 | convolution fusion | flops 4301258752 | bytes 23076864 | tf_op jit(solution)/shard_map/dot_general | solution.py:64
  339.2 17.1 %all-gather.8.cloned.1.call-done = bf16[1024,1024]{1,0:T(8,128)(2,1)} async-done(((bf16[256,1024]{1,0:T(8,128)(2,1)}), bf16[1024,1024]{1,0:T(8,128)(2,1)}) %all-gather.8.cloned.1.call-update) | async-done | bytes 2097168 | tf_op jit(solution)/shard_map/all_gather | solution.py:81
  356.3 10.6 %convolution_bitcast_fusion = f32[2048,1024]{0,1:T(8,128)} fusion(bf16[1024,1024]{1,0:T(8,128)(2,1)} %all-gather.8.cloned.1.call-done, bf16[1024,2048]{1,0:T(8,128)(2,1)} %bitcast.50), kind=kOutput, calls=%fused_computation.4 | convolution fusion | flops 4294967296 | bytes 14680064 | tf_op jit(solution)/shard_map/dot_general | solution.py:82
  366.9 9.4 %copy.13 = f32[2048,1024]{1,0:T(8,128)} copy(f32[2048,1024]{0,1:T(8,128)} %convolution_bitcast_fusion) | data formatting | bytes 16777216
  (40 shorter events, 0.4 us)
Async XLA Ops:
  7.2 255.9 %copy-start = (bf16[1024,1024]{1,0:T(8,128)(2,1)S(1)}, bf16[1024,1024]{1,0:T(8,128)(2,1)}, u32[]{:S(2)}) copy-start(bf16[1024,1024]{1,0:T(8,128)(2,1)} %param.12) | copy-start | bytes 6291460
  7.2 98.6 %reduce-scatter.4.cloned.1.call-start = ((), (), s32[]{:S(2)}) async-start(), calls=%async_computation.5 | async-start | bytes 2621440 | tf_op jit(solution)/shard_map/reduce_scatter | solution.py:27
  7.2 57.8 %slice-start = ((s8[8388608]{0:T(1024)(128)(4,1)}), s8[4194304]{0:T(1024)(128)(4,1)S(1)}, s32[]{:S(2)}) async-start(s8[8388608]{0:T(1024)(128)(4,1)} %bitcast.57), calls=%async_computation.11 | async-start | bytes 8388608
  9.9 55.1 %slice-start.1 = ((s8[8388608]{0:T(1024)(128)(4,1)}), s8[4194304]{0:T(1024)(128)(4,1)S(1)}, s32[]{:S(2)}) async-start(s8[8388608]{0:T(1024)(128)(4,1)} %bitcast.57), calls=%async_computation.12 | async-start | bytes 8388608
  63.0 2.0 copy-start.2
  65.0 40.8 %copy-start.4 = (f32[1024]{0:T(1024)S(1)}, f32[1024]{0:T(1024)}, u32[]{:S(2)}) copy-start(f32[1024]{0:T(1024)} %param.9) | copy-start | bytes 12292
  70.7 73.0 %all-gather.4.cloned.1.call-start = ((), (), s32[]{:S(2)}) async-start(), calls=%async_computation.6 | async-start | bytes 2621440 | tf_op jit(solution)/shard_map/all_gather | solution.py:36
  107.8 96.6 %reduce-scatter.6.cloned.1.call-start = ((), (), s32[]{:S(2)}) async-start(), calls=%async_computation.7 | async-start | bytes 4718592 | tf_op jit(solution)/shard_map/reduce_scatter | solution.py:39
  154.2 50.2 %copy-start.5 = (f32[2048]{0:T(1024)S(1)}, f32[2048]{0:T(1024)}, u32[]{:S(2)}) copy-start(f32[2048]{0:T(1024)} %param.11) | copy-start | bytes 24580
  154.2 97.8 %all-gather.6.cloned.1.call-start = ((), (), s32[]{:S(2)}) async-start(), calls=%async_computation.8 | async-start | bytes 4718592 | tf_op jit(solution)/shard_map/all_gather | solution.py:62
  206.6 56.0 %copy-start.6 = (s32[64]{0:T(128)S(1)}, s32[64]{0:T(128)}, u32[]{:S(2)}) copy-start(s32[64]{0:T(128)} %param.13) | copy-start | bytes 772
  206.6 112.0 %reduce-scatter.8.cloned.1.call-start = ((), (), s32[]{:S(2)}) async-start(), calls=%async_computation.9 | async-start | bytes 2621440 | tf_op jit(solution)/shard_map/reduce_scatter | solution.py:71
  265.0 56.2 %all-to-all-start.1 = ((bf16[4,256,1024]{2,1,0:T(8,128)(2,1)}), bf16[4,256,1024]{2,1,0:T(8,128)(2,1)S(1)}, u32[]{:S(2)}, u32[]{:S(2)}) async-start(bf16[4,256,1024]{2,1,0:T(8,128)(2,1)} %bitcast.47), calls=%async_computation.4 | async-start | bytes 4194304 | tf_op jit(solution)/shard_map/all_to_all | solution.py:101
  268.7 87.6 %all-gather.8.cloned.1.call-start = ((), (), s32[]{:S(2)}) async-start(), calls=%async_computation.10 | async-start | bytes 2621440 | tf_op jit(solution)/shard_map/all_gather | solution.py:81
  268.7 50.0 %copy-start.3 = (bf16[256,1024]{1,0:T(8,128)(2,1)S(1)}, bf16[256,1024]{1,0:T(8,128)(2,1)}, u32[]{:S(2)}) copy-start(bf16[256,1024]{1,0:T(8,128)(2,1)} %reduce-scatter.4.cloned.1.call-done) | copy-start | bytes 1572868
  366.9 9.4 %copy-start.1 = (bf16[1024,1024]{1,0:T(8,128)(2,1)S(1)}, bf16[1024,1024]{1,0:T(8,128)(2,1)}, u32[]{:S(2)}) copy-start(bf16[1024,1024]{1,0:T(8,128)(2,1)} %param.12) | copy-start | bytes 6291460
Sparse Core Ops, SparseCore 0:
  70.8 34.9 reduce-scatter.3
  108.3 35.3 all-gather.3
  154.4 49.9 reduce-scatter.5
  206.7 45.2 all-gather.5
  262.7 55.9 reduce-scatter.7
  320.9 35.2 all-gather.7

commit v2 on v1

v2 whole, which is shorter than its diff:
```python
import functools

import jax
import jax.numpy as jnp
from jax import lax
from jax.experimental import pallas as pl
from jax.experimental.pallas import tpu as pltpu
from jax.sharding import PartitionSpec as P

BLOCK_ROWS = 64
CHUNKS = 4
TILE = 256
MESH = pl.DeviceIdType.MESH

loss_scale = 0.03125
sparsity_weight = 4.0
norm_eps = 1e-06


def rounds_of(latent_count):
    return (latent_count // 2).bit_length() - 1


def kernel(
    nd, nl, chunks,
    paired, enc_w, dec_w, enc_b, dec_b, outgoing,
    col_out, codes_out, err_out, pg_out, norms_out, arrived,
    col, enc16, dec16, stage, part, prec, act, codes, rp, crx, zrx, err, cgp, cgr, pg, sq, sqr,
    local_sem, pair_s, pair_r, fwd_s, fwd_r, pp_s, pp_r, cd_s, cd_r, cx_s, cx_r, zx_s, zx_r,
    za_s, za_r, ca_s, ca_r, cg_s, cg_r, pg_s, pg_r, sq_s, sq_r, bf_s, bf_r, own_sem, out_sem,
):
    f32, bf16 = jnp.float32, jnp.bfloat16
    rows = paired.shape[0] // chunks
    feats, lats = enc_w.shape
    m = rows * nd
    half = feats // 2
    nb = rounds_of(nl)
    me = lax.axis_index("dp")
    li = lax.axis_index("latent")
    zi = lax.div(li, 2)
    core = lax.rem(li, 2)
    mate = {"latent": li + 1 - 2 * core}
    bits = [lax.rem(lax.div(zi, 1 << b), 2) for b in range(nb)]
    zpeer = [{"latent": li + (2 << b) * (1 - 2 * bits[b])} for b in range(nb)]
    ahead = [lax.rem(me + k, nd) for k in range(nd)]
    behind = [lax.rem(me + nd - k, nd) for k in range(nd)]
    dpeer = [{"dp": ahead[k]} for k in range(nd)]

    def at_rows(index, size):
        return pl.ds(pl.multiple_of(index, 16), size)

    my_rows = at_rows(me * rows, rows)

    def remote(src, dst, s, r, dev):
        return pltpu.make_async_remote_copy(
            src_ref=src, dst_ref=dst, send_sem=s, recv_sem=r, device_id=dev, device_id_type=MESH
        )

    enc_copy = pltpu.make_async_copy(enc_w, stage, local_sem.at[0])
    enc_copy.start()

    barrier = pltpu.get_barrier_semaphore()
    friends = dpeer[1:] + [mate] + zpeer
    for dev in friends:
        pl.semaphore_signal(barrier, inc=1, device_id=dev, device_id_type=MESH)
    pl.semaphore_wait(barrier, len(friends))

    sends = []

    def go(copy):
        copy.start()
        sends.append(copy)
        return copy

    my_half = pl.ds(pl.multiple_of(core * half, 128), half)
    pair_copies, fwd_copies, own_copies = {}, {}, {}
    for c in range(chunks):
        for k in range(1, nd):
            source = pl.ds(pl.multiple_of(ahead[k] * feats + core * half, 128), half)
            pair_copies[c, k] = go(remote(
                paired.at[pl.ds(c * rows, rows), source],
                col.at[c, my_rows, my_half],
                pair_s.at[c, k - 1], pair_r.at[c, k - 1], dpeer[k],
            ))
        own_copies[c] = pltpu.make_async_copy(
            paired.at[pl.ds(c * rows, rows), pl.ds(pl.multiple_of(me * feats, 128), feats)],
            col.at[c, my_rows],
            own_sem.at[c],
        )
        own_copies[c].start()
    own_block = pltpu.make_async_copy(outgoing.at[me], arrived.at[me], local_sem.at[2])
    own_block.start()

    enc_copy.wait()

    @pl.loop(0, feats // 128)
    def _(i):
        r = pl.ds(pl.multiple_of(i * 128, 128), 128)
        enc16[r, :] = stage[r, :].astype(bf16)

    def forward(c):
        for k in range(1, nd):
            pair_copies[c, k].wait_recv()
            block = col.at[c, at_rows(behind[k] * rows, rows), my_half]
            fwd_copies[c, k] = go(remote(block, block, fwd_s.at[c, k - 1], fwd_r.at[c, k - 1], mate))

    pp_copies, cd_copies, cx_copies, zx_copies = {}, {}, {}, {}
    za_copies, ca_copies, cg_copies, pg_copies = {}, {}, {}, {}

    def encode(c):
        own_copies[c].wait()
        for k in range(1, nd):
            fwd_copies[c, k].wait_recv()

        @pl.loop(0, lats // TILE)
        def _(j):
            t = pl.ds(pl.multiple_of(j * TILE, TILE), TILE)
            part[c, :, t] = jnp.dot(col[c], enc16[:, t], preferred_element_type=f32).astype(bf16)

        for k in range(1, nd):
            pp_copies[c, k] = go(remote(
                part.at[c, at_rows(ahead[k] * rows, rows)], prec.at[c, k - 1],
                pp_s.at[c, k - 1], pp_r.at[c, k - 1], dpeer[k],
            ))

    def activate(c):
        for k in range(1, nd):
            pp_copies[c, k].wait_recv()
        total = part[c, my_rows, :].astype(f32)
        for k in range(1, nd):
            total = total + prec[c, k - 1].astype(f32)
        a = jnp.maximum(total + enc_b[...], 0.0)
        act[c] = a
        codes[c, my_rows, :] = (a * a).astype(bf16)
        for k in range(1, nd):
            block = codes.at[c, my_rows]
            cd_copies[c, k] = go(remote(block, block, cd_s.at[c, k - 1], cd_r.at[c, k - 1], dpeer[k]))

    def decode(c):
        for k in range(1, nd):
            cd_copies[c, k].wait_recv()

        @pl.loop(0, feats // TILE)
        def _(j):
            t = pl.ds(pl.multiple_of(j * TILE, TILE), TILE)
            rp[c, :, t] = jnp.dot(codes[c], dec16[:, t], preferred_element_type=f32).astype(bf16)

        cx_copies[c] = go(remote(
            rp.at[c, at_rows((1 - core) * (m // 2), m // 2)], crx.at[c], cx_s.at[c], cx_r.at[c], mate
        ))

    bases, sizes = [core * (m // 2)], [m // 2]
    for b in range(nb):
        sizes.append(sizes[-1] // 2)
        bases.append(bases[-1] + bits[b] * sizes[-1])
    zoff = [0]
    for b in range(nb):
        zoff.append(zoff[-1] + sizes[b + 1])

    def add_rows(c, base, size, source, start):
        @pl.loop(0, size // 32)
        def _(i):
            r = at_rows(base + i * 32, 32)
            s = at_rows(start + i * 32, 32)
            rp[c, r, :] = (rp[c, r, :].astype(f32) + source[c, s, :].astype(f32)).astype(bf16)

    def halve(b, c):
        if b == 0:
            cx_copies[c].wait_recv()
            add_rows(c, bases[0], sizes[0], crx, 0)
        else:
            zx_copies[c, b - 1].wait_recv()
            add_rows(c, bases[b], sizes[b], zrx, zoff[b - 1])
        size = sizes[b + 1]
        zx_copies[c, b] = go(remote(
            rp.at[c, at_rows(bases[b] + (1 - bits[b]) * size, size)],
            zrx.at[c, pl.ds(zoff[b], size)],
            zx_s.at[c, b], zx_r.at[c, b], zpeer[b],
        ))

    def spread(b, c):
        block = err.at[c, at_rows(bases[b + 1], sizes[b + 1])]
        za_copies[c, b] = go(remote(block, block, za_s.at[c, b], za_r.at[c, b], zpeer[b]))

    def error(c):
        b = nb - 1
        zx_copies[c, b].wait_recv()

        @pl.loop(0, sizes[nb] // 32)
        def _(i):
            r = at_rows(bases[nb] + i * 32, 32)
            s = at_rows(zoff[b] + i * 32, 32)
            recon = rp[c, r, :].astype(f32) + zrx[c, s, :].astype(f32) + dec_b[...]
            err[c, r, :] = (2.0 * loss_scale * (recon - col[c, r, :].astype(f32))).astype(bf16)

        spread(b, c)

    def widen(b, c):
        za_copies[c, b + 1].wait_recv()
        spread(b, c)

    def share(c):
        za_copies[c, 0].wait_recv()
        block = err.at[c, at_rows(bases[0], m // 2)]
        ca_copies[c] = go(remote(block, block, ca_s.at[c], ca_r.at[c], mate))

    def back(c):
        ca_copies[c].wait_recv()

        @pl.loop(0, lats // TILE)
        def _(j):
            t = pl.ds(pl.multiple_of(j * TILE, TILE), TILE)
            cgp[c, :, t] = lax.dot_general(
                err[c], dec16[t, :], (((1,), (1,)), ((), ())), preferred_element_type=f32
            ).astype(bf16)

        for k in range(1, nd):
            cg_copies[c, k] = go(remote(
                cgp.at[c, at_rows(ahead[k] * rows, rows)], cgr.at[c, k - 1],
                cg_s.at[c, k - 1], cg_r.at[c, k - 1], dpeer[k],
            ))

    def grad(c):
        for k in range(1, nd):
            cg_copies[c, k].wait_recv()
        total = cgp[c, my_rows, :].astype(f32)
        for k in range(1, nd):
            total = total + cgr[c, k - 1].astype(f32)
        penalty = sparsity_weight * loss_scale * (sq[1, 0:1, :] + sq[2, 0:1, :])
        pg[c, my_rows, :] = ((total + penalty) * 2.0 * act[c]).astype(bf16)
        for k in range(1, nd):
            block = pg.at[c, my_rows]
            pg_copies[c, k] = go(remote(block, block, pg_s.at[c, k - 1], pg_r.at[c, k - 1], dpeer[k]))

    outs = []

    def finish(c):
        for k in range(1, nd):
            pg_copies[c, k].wait_recv()
        copy = pltpu.make_async_copy(pg.at[c], pg_out.at[c], out_sem.at[c])
        copy.start()
        outs.append(copy)

    forward(0)
    dec_copies = []
    for h in range(feats // lats):
        copy = pltpu.make_async_copy(
            dec_w.at[:, pl.ds(h * lats, lats)], stage.at[pl.ds(h * lats, lats)], local_sem.at[3 + h]
        )
        copy.start()
        dec_copies.append(copy)
    for copy in dec_copies:
        copy.wait()

    @pl.loop(0, lats // 128)
    def _(i):
        acc = jnp.zeros((128, 128), f32)
        r = pl.ds(pl.multiple_of(i * 128, 128), 128)
        for h in range(feats // lats):
            x = stage[pl.ds(pl.multiple_of(h * lats + i * 128, 128), 128), :]
            dec16[r, pl.ds(h * lats, lats)] = x.astype(bf16)
            for q in range(lats // 128):
                y = x[:, q * 128:(q + 1) * 128]
                acc = acc + y * y
        line = jnp.sum(acc.T, axis=0, keepdims=True)
        sq[0, :, r] = jnp.broadcast_to(line, (8, 128))

    sq_copies = [
        go(remote(sq.at[0], sqr.at[k - 1], sq_s.at[k - 1], sq_r.at[k - 1], dpeer[k]))
        for k in range(1, nd)
    ]

    def norms():
        for copy in sq_copies:
            copy.wait_recv()
        mine = sq[0]
        first = jnp.where(me < nd // 2, mine, 0.0)
        second = mine - first
        for k in range(1, nd):
            x = sqr[k - 1]
            low = jnp.where(behind[k] < nd // 2, x, 0.0)
            first, second = first + low, second + (x - low)
        sq[1] = jnp.sqrt(first + norm_eps)
        sq[2] = jnp.sqrt(second + norm_eps)
        copy = pltpu.make_async_copy(sq.at[pl.ds(1, 2)], norms_out, local_sem.at[1])
        copy.start()
        outs.append(copy)

    bf_copies = []

    def send_buffer():
        for k in range(1, nd):
            bf_copies.append(go(remote(
                outgoing.at[ahead[k]], arrived.at[me], bf_s.at[k - 1], bf_r.at[k - 1], dpeer[k]
            )))

    def put(ref, out, base, c):
        copy = pltpu.make_async_copy(ref.at[c], out.at[c], out_sem.at[base * chunks + c])
        copy.start()
        outs.append(copy)

    steps = [forward, encode, activate, decode]
    steps += [functools.partial(halve, b) for b in range(nb)]
    steps += [error]
    steps += [functools.partial(widen, b) for b in reversed(range(nb - 1))]
    steps += [share, back, grad, finish]
    lead = 1
    for t in range(len(steps) + lead * (chunks - 1)):
        for c in range(chunks):
            s = t - lead * c
            if 0 <= s < len(steps) and not (s == 0 and c == 0):
                steps[s](c)
                if s == 3:
                    put(col, col_out, 1, c)
                    put(codes, codes_out, 2, c)
                if steps[s] is back:
                    put(err, err_out, 3, c)
                if s == 2 and c == chunks - 1:
                    send_buffer()
                if s == 4 and c == 0:
                    norms()
    for copy in bf_copies:
        copy.wait_recv()
    own_block.wait()
    for copy in outs:
        copy.wait()
    for copy in sends:
        copy.wait_send()


def exchange(nd, nl, paired, enc_weight, dec_weight, enc_bias, dec_bias, outgoing):
    chunks = CHUNKS
    rows = paired.shape[0] // chunks
    feats, lats = enc_weight.shape
    m = rows * nd
    nb = rounds_of(nl)
    bf16, f32 = jnp.bfloat16, jnp.float32
    hbm = pl.BlockSpec(memory_space=pl.ANY)
    vmem = pl.BlockSpec(memory_space=pltpu.VMEM)
    dma = pltpu.SemaphoreType.DMA
    peers = nd - 1
    big = [(chunks, m, feats), (chunks, m, lats)]
    pair = [dma((chunks, peers)), dma((chunks, peers))]
    single = [dma((chunks,)), dma((chunks,))]
    zs = [dma((chunks, nb)), dma((chunks, nb))]
    flops = 3 * 2 * chunks * m * feats * lats
    return pl.pallas_call(
        functools.partial(kernel, nd, nl, chunks),
        out_shape=(
            jax.ShapeDtypeStruct(big[0], bf16),
            jax.ShapeDtypeStruct(big[1], bf16),
            jax.ShapeDtypeStruct(big[0], bf16),
            jax.ShapeDtypeStruct(big[1], bf16),
            jax.ShapeDtypeStruct((2, 8, lats), f32),
            jax.ShapeDtypeStruct(outgoing.shape, bf16),
        ),
        in_specs=[hbm, hbm, hbm, vmem, vmem, hbm],
        out_specs=(hbm,) * 6,
        scratch_shapes=[
            pltpu.VMEM(big[0], bf16),
            pltpu.VMEM((feats, lats), bf16),
            pltpu.VMEM((lats, feats), bf16),
            pltpu.VMEM((feats, lats), f32),
            pltpu.VMEM(big[1], bf16),
            pltpu.VMEM((chunks, peers, rows, lats), bf16),
            pltpu.VMEM((chunks, rows, lats), f32),
            pltpu.VMEM(big[1], bf16),
            pltpu.VMEM(big[0], bf16),
            pltpu.VMEM((chunks, m // 2, feats), bf16),
            pltpu.VMEM((chunks, m // 2, feats), bf16),
            pltpu.VMEM(big[0], bf16),
            pltpu.VMEM(big[1], bf16),
            pltpu.VMEM((chunks, peers, rows, lats), bf16),
            pltpu.VMEM(big[1], bf16),
            pltpu.VMEM((3, 8, lats), f32),
            pltpu.VMEM((peers, 8, lats), f32),
            dma((8,)),
            *pair, *pair, *pair, *pair, *single, *zs, *zs, *single, *pair, *pair,
            dma((peers,)), dma((peers,)), dma((peers,)), dma((peers,)),
            dma((chunks,)), dma((4 * chunks,)),
        ],
        compiler_params=pltpu.CompilerParams(
            collective_id=0, has_side_effects=True, vmem_limit_bytes=60 * 1024 * 1024
        ),
        cost_estimate=pl.CostEstimate(flops=flops, bytes_accessed=40 << 20, transcendentals=0),
    )(paired, enc_weight, dec_weight, enc_bias[None, :], dec_bias[None, :], outgoing)


def body(paired, enc_weight, enc_bias, dec_weight, dec_bias, buffer_rows, block_dest):
    data_count = lax.axis_size("dp")
    latent_count = lax.axis_size("latent")
    data_index = lax.axis_index("dp")
    contract_rows = (((0,), (0,)), ((), ()))
    blocks_here = buffer_rows.shape[0] // BLOCK_ROWS
    per_device = blocks_here // data_count
    block_iota = jnp.arange(blocks_here, dtype=jnp.int32)
    own_dest = lax.dynamic_slice_in_dim(block_dest, data_index * blocks_here, blocks_here, 0)
    target_device = own_dest // blocks_here
    earlier_same = (target_device[None, :] == target_device[:, None]) & (
        own_dest[None, :] < own_dest[:, None]
    )
    send_slot = target_device * per_device + jnp.sum(earlier_same.astype(jnp.int32), axis=1)
    chosen = jnp.sum(
        jnp.where(send_slot[None, :] == block_iota[:, None], block_iota[None, :], 0), axis=1
    )
    feature_count = buffer_rows.shape[1]
    outgoing = buffer_rows.reshape(blocks_here, BLOCK_ROWS, feature_count)[chosen].reshape(
        data_count, buffer_rows.shape[0] // data_count, feature_count
    )
    col, codes, err, pg, norms, arrived = exchange(
        data_count, latent_count, paired, enc_weight, dec_weight, enc_bias, dec_bias, outgoing
    )
    feats, lats = enc_weight.shape
    col, err = col.reshape(-1, feats), err.reshape(-1, feats)
    codes, pg = codes.reshape(-1, lats), pg.reshape(-1, lats)
    enc_grad = lax.dot_general(col, pg, contract_rows, preferred_element_type=jnp.float32)
    model_index = data_index // (data_count // 2)
    own_norm = jnp.where(model_index == 0, norms[0, 0], norms[1, 0])
    code_sum = jnp.sum(codes, axis=0, dtype=jnp.float32)
    dec_main = lax.dot_general(codes, err, contract_rows, preferred_element_type=jnp.float32)
    dec_grad = (
        dec_main + sparsity_weight * loss_scale * code_sum[:, None] * dec_weight / own_norm[:, None]
    )
    positions = data_index * blocks_here + block_iota
    every_block = jnp.arange(block_dest.shape[0], dtype=jnp.int32)
    source_block = jnp.sum(
        jnp.where(block_dest[None, :] == positions[:, None], every_block[None, :], 0), axis=1
    )
    sender_device = source_block // blocks_here
    before_same = (sender_device[None, :] == sender_device[:, None]) & (
        block_iota[None, :] < block_iota[:, None]
    )
    arrival_slot = sender_device * per_device + jnp.sum(before_same.astype(jnp.int32), axis=1)
    shuffled = arrived.reshape(blocks_here, BLOCK_ROWS, feature_count)[arrival_slot].reshape(
        buffer_rows.shape
    )
    return (enc_grad, dec_grad, shuffled)


def solution(mesh):
    in_specs = (
        P("dp", None),
        P("dp", "latent"),
        P("latent"),
        P("latent", "dp"),
        P("dp"),
        P("dp", "latent"),
        P(),
    )
    out_specs = (P("dp", "latent"), P("latent", "dp"), P("dp", "latent"))
    return jax.shard_map(body, mesh=mesh, in_specs=in_specs, out_specs=out_specs, check_vma=False)
```

time: 384 us -> 206 us (0.54)
  waiting for transfers between devices: 195 us -> 0 us
  Pallas kernels: 0 us -> 170 us
  blocking collectives: 87.5 us -> 0 us
  matrix products: 51.2 us -> 24.2 us
  between operations: 14.3 us -> 0.69 us
  local copies, waits for them, and re-layouts: 18.1 us -> 6.18 us
  other arithmetic: 13.2 us -> 5.01 us
  starting transfers between devices: 3.89 us -> 0 us
    pallas_call x0 -> x1, Pallas kernels: none -> 170 us  [exchange(): pl.pallas_call(functools.partial(kernel, nd, nl, chunks), out_shape=(jax....]
    all_gather x3 -> x0, waiting for transfers between devices: 98.3 us -> none  [the longest x1 45.4 us: body(): all_errors = lax.all_gather(error_grad, 'latent', axis=0, tiled=True)]
    reduce_scatter x3 -> x0, waiting for transfers between devices: 96.5 us -> none  [the longest x1 50.1 us: body(): lax.psum_scatter(jnp.dot(row_block, dec16, preferred_element_type=jnp.flo...]
    all_to_all x1 -> x0, blocking collectives: 53.1 us -> none  [body(): lax.all_to_all(paired, 'dp', split_axis=1, concat_axis=0, tiled=True)]
    psum x1 -> x0, blocking collectives: 34.4 us -> none  [body(): square_sums = lax.psum(square_pair, 'dp')]
    dot_general x5 -> x2, matrix products: 51.2 us -> 24.2 us  [the longest x1 13.4 us: body(): lax.dot_general(codes, err, contract_rows, preferred_element_type=jnp.flo...]
    unnamed x19 -> x2, local copies, waits for them, and re-layouts: 11.4 us -> 0.6 us
    convert_element_type x3 -> x0, other arithmetic: 6.3 us -> none  [the longest x1 2.19 us: body(): error_grad = (2.0 * loss_scale * recon_error).astype(jnp.bfloat16)]
  transfers between devices with their start and end apart: 7 -> 0, of which waited for: 6 -> 0; matrix products, arithmetic and copies ran while one was open for 7% -> 0% of each run, Pallas kernels for 0% -> 0%
where the time goes in v2:
time: 206 us
  Pallas kernels  170 us (83%)
  matrix products  24.2 us (12%)
  local copies, waits for them, and re-layouts  6.18 us (3%)
  other arithmetic  5.01 us (2%)
    pallas_call x1, Pallas kernels, exchange(): pl.pallas_call(functools.partial(kernel, nd, nl, chunks), out_shape=(jax....  170 us
    dot_general x1, matrix products, body(): lax.dot_general(codes, err, contract_rows, preferred_element_type=jnp.flo...  13.4 us
    dot_general x1, matrix products, body(): lax.dot_general(col, pg, contract_rows, preferred_element_type=jnp.float32)  10.8 us

profile of v2, /device:TPU:0, one launch (start us, length us, event | category | flops | bytes accessed | tf_op | source)
XLA Modules:
  0.0 206.0 jit_solution(10826313196560437790)
XLA Ops:
  0.6 0.0 copy-start
  0.7 1.0 select_reduce_fusion
  1.7 0.6 copy-done
  2.3 0.2 convert_reduce_fusion.1
  2.5 0.7 and_select_fusion.2
  3.2 0.2 convert_reduce_fusion.2
  3.4 0.1 select_reduce_fusion.1
  3.5 2.0 gather_fusion
  5.5 169.9 %shard_map.94 = (bf16[4,256,2048]{2,1,0:T(8,128)(2,1)}, bf16[4,256,1024]{2,1,0:T(8,128)(2,1)}, bf16[4,256,2048]{2,1,0:T(8,128)(2,1)}, bf16[4,256,1024]{2,1,0:T(8...) custom-call(bf16[256,8192]{1,0:T(8,128)(2,1)} %paired.1, f32[2048,1024]{1,0:T(8,128)} %enc_w.1, ...), custom_call_target="tpu_custom_call" | custom-call | flops 12884901888 | bytes 41943040 | tf_op jit(solution)/shard_map/pallas_call | solution.py:347
  175.4 0.8 broadcast_select_fusion
  176.2 2.0 convert_reduce_fusion
  178.2 13.4 %bitcast_add_fusion = f32[1024,2048]{1,0:T(8,128)} fusion(f32[1024,2048]{1,0:T(8,128)} %dec_w.1, bf16[4,256,1024]{2,1,0:T(8,128)(2,1)} %get-tuple-element.11, bf16[4,256,2048]{2,1,0:T(8,128)(2,1)} %get-tuple-element.12, f32[1024]{0:T(1024)S(1)} %bitcast.39, f32[1024]{0:T(1024)S(1)} %broadcast_multiply_fusion), kind=kOutput, calls=%fused_computation.2 | convolution fusion | flops 4301258752 | bytes 23076864 | tf_op jit(solution)/shard_map/dot_general | solution.py:420
  191.5 3.6 %gather_fusion.1 = bf16[16,64,1024]{2,1,0:T(8,128)(2,1)} fusion(bf16[16,64,1024]{2,1,0:T(8,128)(2,1)} %bitcast.36, s32[1024]{0:T(1024)S(1)} %pad_clamp_fusion), kind=kCustom, calls=%fused_computation.1 | custom fusion | bytes 4194368 | tf_op jit(solution)/shard_map/gather | solution.py:434
  195.1 10.8 %convolution_bitcast_fusion = f32[2048,1024]{1,0:T(8,128)} fusion(bf16[4,256,2048]{2,1,0:T(8,128)(2,1)} %get-tuple-element.9, bf16[4,256,1024]{2,1,0:T(8,128)(2,1)} %get-tuple-element.10), kind=kOutput, calls=%fused_computation.3 | convolution fusion | flops 4294967296 | bytes 14680064 | tf_op jit(solution)/shard_map/dot_general | solution.py:416
  (8 shorter events, 0.1 us)
Async XLA Ops:
  0.6 1.6 copy-start

commit v3 on v2

--- a/solution.py
+++ b/solution.py
@@ -24,10 +24,10 @@
 def kernel(
     nd, nl, chunks,
     paired, enc_w, dec_w, enc_b, dec_b, outgoing,
-    col_out, codes_out, err_out, pg_out, norms_out, arrived,
-    col, enc16, dec16, stage, part, prec, act, codes, rp, crx, zrx, err, cgp, cgr, pg, sq, sqr,
+    col_out, pg_out, dec_out, arrived,
+    col, enc16, dec16, stage, part, prec, act, codes, rp, crx, zrx, err, cgp, cgr, pg, sq, sqr, codest, scale, dtile,
     local_sem, pair_s, pair_r, fwd_s, fwd_r, pp_s, pp_r, cd_s, cd_r, cx_s, cx_r, zx_s, zx_r,
-    za_s, za_r, ca_s, ca_r, cg_s, cg_r, pg_s, pg_r, sq_s, sq_r, bf_s, bf_r, own_sem, out_sem,
+    za_s, za_r, ca_s, ca_r, cg_s, cg_r, pg_s, pg_r, sq_s, sq_r, bf_s, bf_r, own_sem, out_sem, tile_sem,
 ):
     f32, bf16 = jnp.float32, jnp.bfloat16
     rows = paired.shape[0] // chunks
@@ -74,7 +74,7 @@
 
     my_half = pl.ds(pl.multiple_of(core * half, 128), half)
     pair_copies, fwd_copies, own_copies = {}, {}, {}
-    for c in range(chunks):
+    def send_pair(c):
         for k in range(1, nd):
             source = pl.ds(pl.multiple_of(ahead[k] * feats + core * half, 128), half)
             pair_copies[c, k] = go(remote(
@@ -88,6 +88,9 @@
             own_sem.at[c],
         )
         own_copies[c].start()
+
+    for c in range(1):
+        send_pair(c)
     own_block = pltpu.make_async_copy(outgoing.at[me], arrived.at[me], local_sem.at[2])
     own_block.start()
 
@@ -148,6 +151,11 @@
         cx_copies[c] = go(remote(
             rp.at[c, at_rows((1 - core) * (m // 2), m // 2)], crx.at[c], cx_s.at[c], cx_r.at[c], mate
         ))
+
+        @pl.loop(0, lats // TILE)
+        def _(j):
+            t = pl.ds(pl.multiple_of(j * TILE, TILE), TILE)
+            codest[t, pl.ds(c * m, m)] = codes[c, :, t].T
 
     bases, sizes = [core * (m // 2)], [m // 2]
     for b in range(nb):
@@ -282,9 +290,46 @@
             first, second = first + low, second + (x - low)
         sq[1] = jnp.sqrt(first + norm_eps)
         sq[2] = jnp.sqrt(second + norm_eps)
-        copy = pltpu.make_async_copy(sq.at[pl.ds(1, 2)], norms_out, local_sem.at[1])
+
+    def scales():
+        @pl.loop(0, lats // 128)
+        def _(i):
+            r = pl.ds(pl.multiple_of(i * 128, 128), 128)
+            total = jnp.sum(codest[r, :].astype(f32), axis=1, keepdims=True)
+            norm = jnp.where(me < nd // 2, sq[1, 0:1, r], sq[2, 0:1, r])
+            spread_norm = jnp.broadcast_to(norm, (128, 128)).T
+            scale[r, :] = sparsity_weight * loss_scale * total / spread_norm
+
+    tiles = []
+
+    def dec_tile(j):
+        slot = j % 2
+        if j >= 2:
+            tiles[j - 2].wait()
+        start = (j * TILE // lats) * lats
+        lane = j * TILE % lats
+
+        @pl.loop(0, lats // 256)
+        def _(i):
+            r = pl.ds(pl.multiple_of(i * 256, 256), 256)
+            w = pl.ds(pl.multiple_of(start + i * 256, 256), 256)
+            acc = jnp.zeros((256, TILE), f32)
+            for c in range(chunks):
+                acc = acc + jnp.dot(
+                    codest[r, c * m:(c + 1) * m], err[c, :, j * TILE:(j + 1) * TILE],
+                    preferred_element_type=f32,
+                )
+            for q in range(TILE // 128):
+                dtile[slot, r, q * 128:(q + 1) * 128] = (
+                    acc[:, q * 128:(q + 1) * 128]
+                    + scale[r, :] * stage[w, lane + q * 128:lane + (q + 1) * 128]
+                )
+
+        copy = pltpu.make_async_copy(
+            dtile.at[slot], dec_out.at[:, pl.ds(j * TILE, TILE)], tile_sem.at[slot]
+        )
         copy.start()
-        outs.append(copy)
+        tiles.append(copy)
 
     bf_copies = []
 
@@ -304,24 +349,36 @@
     steps += [error]
     steps += [functools.partial(widen, b) for b in reversed(range(nb - 1))]
     steps += [share, back, grad, finish]
-    lead = 1
+    lead = 2
+    count = feats // TILE
+    sent = [1]
     for t in range(len(steps) + lead * (chunks - 1)):
-        for c in range(chunks):
+        while sent[0] < chunks and t >= lead * sent[0] - 2:
+            send_pair(sent[0])
+            sent[0] += 1
+        for c in reversed(range(chunks)):
             s = t - lead * c
             if 0 <= s < len(steps) and not (s == 0 and c == 0):
                 steps[s](c)
                 if s == 3:
                     put(col, col_out, 1, c)
-                    put(codes, codes_out, 2, c)
-                if steps[s] is back:
-                    put(err, err_out, 3, c)
+                    if c == chunks - 1:
+                        scales()
                 if s == 2 and c == chunks - 1:
                     send_buffer()
-                if s == 4 and c == 0:
+                if s == 2 and c == 1:
                     norms()
+                if c == chunks - 1 and steps[s] is back:
+                    for j in range(count // 2):
+                        dec_tile(j)
+                if c == chunks - 1 and steps[s] is grad:
+                    for j in range(count // 2, count):
+                        dec_tile(j)
     for copy in bf_copies:
         copy.wait_recv()
     own_block.wait()
+    for copy in tiles[-2:]:
+        copy.wait()
     for copy in outs:
         copy.wait()
     for copy in sends:
@@ -349,13 +406,11 @@
         out_shape=(
             jax.ShapeDtypeStruct(big[0], bf16),
             jax.ShapeDtypeStruct(big[1], bf16),
-            jax.ShapeDtypeStruct(big[0], bf16),
-            jax.ShapeDtypeStruct(big[1], bf16),
-            jax.ShapeDtypeStruct((2, 8, lats), f32),
+            jax.ShapeDtypeStruct((lats, feats), f32),
             jax.ShapeDtypeStruct(outgoing.shape, bf16),
         ),
         in_specs=[hbm, hbm, hbm, vmem, vmem, hbm],
-        out_specs=(hbm,) * 6,
+        out_specs=(hbm,) * 4,
         scratch_shapes=[
             pltpu.VMEM(big[0], bf16),
             pltpu.VMEM((feats, lats), bf16),
@@ -374,10 +429,13 @@
             pltpu.VMEM(big[1], bf16),
             pltpu.VMEM((3, 8, lats), f32),
             pltpu.VMEM((peers, 8, lats), f32),
+            pltpu.VMEM((lats, chunks * m), bf16),
+            pltpu.VMEM((lats, 128), f32),
+            pltpu.VMEM((2, lats, TILE), f32),
             dma((8,)),
             *pair, *pair, *pair, *pair, *single, *zs, *zs, *single, *pair, *pair,
             dma((peers,)), dma((peers,)), dma((peers,)), dma((peers,)),
-            dma((chunks,)), dma((4 * chunks,)),
+            dma((chunks,)), dma((2 * chunks,)), dma((2,)),
         ],
         compiler_params=pltpu.CompilerParams(
             collective_id=0, has_side_effects=True, vmem_limit_bytes=60 * 1024 * 1024
@@ -407,19 +465,13 @@
     outgoing = buffer_rows.reshape(blocks_here, BLOCK_ROWS, feature_count)[chosen].reshape(
         data_count, buffer_rows.shape[0] // data_count, feature_count
     )
-    col, codes, err, pg, norms, arrived = exchange(
+    col, pg, dec_grad, arrived = exchange(
         data_count, latent_count, paired, enc_weight, dec_weight, enc_bias, dec_bias, outgoing
     )
     feats, lats = enc_weight.shape
-    col, err = col.reshape(-1, feats), err.reshape(-1, feats)
-    codes, pg = codes.reshape(-1, lats), pg.reshape(-1, lats)
-    enc_grad = lax.dot_general(col, pg, contract_rows, preferred_element_type=jnp.float32)
-    model_index = data_index // (data_count // 2)
-    own_norm = jnp.where(model_index == 0, norms[0, 0], norms[1, 0])
-    code_sum = jnp.sum(codes, axis=0, dtype=jnp.float32)
-    dec_main = lax.dot_general(codes, err, contract_rows, preferred_element_type=jnp.float32)
-    dec_grad = (
-        dec_main + sparsity_weight * loss_scale * code_sum[:, None] * dec_weight / own_norm[:, None]
+    enc_grad = lax.dot_general(
+        col.reshape(-1, feats), pg.reshape(-1, lats), contract_rows,
+        preferred_element_type=jnp.float32,
     )
     positions = data_index * blocks_here + block_iota
     every_block = jnp.arange(block_dest.shape[0], dtype=jnp.int32)

time: 206 us -> 186 us (0.903)
  matrix products: 24.2 us -> 11 us
  Pallas kernels: 170 us -> 162 us
  local copies, waits for them, and re-layouts: 6.18 us -> 9.6 us
  other arithmetic: 5.01 us -> 2.26 us
    dot_general x2 -> x1, matrix products: 24.2 us -> 11 us  [body(): lax.dot_general(col.reshape(-1, feats), pg.reshape(-1, lats), contract_ro...]
    pallas_call x1, Pallas kernels: 170 us -> 162 us  [exchange(): pl.pallas_call(functools.partial(kernel, nd, nl, chunks), out_shape=(jax....]
    unnamed x2 -> x5, local copies, waits for them, and re-layouts: 0.6 us -> 4.01 us
where the time goes in v3:
time: 186 us
  Pallas kernels  162 us (87%)
  matrix products  11 us (6%)
  local copies, waits for them, and re-layouts  9.6 us (5%)
  other arithmetic  2.26 us (1%)
    pallas_call x1, Pallas kernels, exchange(): pl.pallas_call(functools.partial(kernel, nd, nl, chunks), out_shape=(jax....  162 us
    dot_general x1, matrix products, body(): lax.dot_general(col.reshape(-1, feats), pg.reshape(-1, lats), contract_ro...  11 us
    unnamed x5, local copies, waits for them, and re-layouts  4.01 us

profile of v3, /device:TPU:0, one launch (start us, length us, event | category | flops | bytes accessed | tf_op | source)
XLA Modules:
  0.0 185.8 jit_solution(17684220296304853316)
XLA Ops:
  0.6 0.0 copy-start
  0.7 1.0 select_reduce_fusion
  1.6 0.6 copy-done
  2.3 0.2 convert_reduce_fusion
  2.5 0.7 and_select_fusion.2
  3.2 0.2 convert_reduce_fusion.1
  3.4 0.1 select_reduce_fusion.1
  3.5 2.0 %gather_fusion = bf16[16,64,1024]{2,1,0:T(8,128)(2,1)} fusion(bf16[16,64,1024]{2,1,0:T(8,128)(2,1)S(1)} %bitcast.30, s32[1024]{0:T(1024)S(1)} %pad_clamp_fusion.1), kind=kCustom, calls=%fused_computation | custom fusion | bytes 4194368 | tf_op jit(solution)/shard_map/gather | solution.py:465
  5.5 162.3 %shard_map.94 = (bf16[4,256,2048]{2,1,0:T(8,128)(2,1)}, bf16[4,256,1024]{2,1,0:T(8,128)(2,1)}, f32[1024,2048]{1,0:T(8,128)}, bf16[4,256,1024]{2,1,0:T(8,128)(2,1)}) custom-call(bf16[256,8192]{1,0:T(8,128)(2,1)} %paired.1, f32[2048,1024]{1,0:T(8,128)} %enc_w.1, f32[1024,2048]{1,0:T(8,128)} %dec_w.1, f32[1,1024]{1,0:T(1,128)} %bitcast.35, f32[1,2048]{1,0:T(1,128)} %bitcast.34, ...), custom_call_target="tpu_custom_call" | custom-call | flops 12884901888 | bytes 41943040 | tf_op jit(solution)/shard_map/pallas_call | solution.py:404
  167.8 3.6 %gather_fusion.1 = bf16[16,64,1024]{2,1,0:T(8,128)(2,1)} fusion(bf16[16,64,1024]{2,1,0:T(8,128)(2,1)} %bitcast.32, s32[1024]{0:T(1024)S(1)} %pad_clamp_fusion), kind=kCustom, calls=%fused_computation.1 | custom fusion | bytes 4194368 | tf_op jit(solution)/shard_map/gather | solution.py:486
  171.4 0.0 copy-start.1
  171.4 11.0 %convolution_bitcast_fusion = f32[2048,1024]{1,0:T(8,128)} fusion(bf16[4,256,2048]{2,1,0:T(8,128)(2,1)} %get-tuple-element.7, bf16[4,256,1024]{2,1,0:T(8,128)(2,1)} %get-tuple-element.8), kind=kOutput, calls=%fused_computation.2 | convolution fusion | flops 4294967296 | bytes 14680064 | tf_op jit(solution)/shard_map/dot_general | solution.py:472
  182.4 0.0 copy-done.1
  182.4 3.4 %copy.14 = f32[1024,2048]{1,0:T(8,128)} copy(f32[1024,2048]{1,0:T(8,128)S(1)} %copy-done.1) | data formatting | bytes 16777216
  (7 shorter events, 0.1 us)
Async XLA Ops:
  0.6 1.6 copy-start
  171.4 11.0 %copy-start.1 = (f32[1024,2048]{1,0:T(8,128)S(1)}, f32[1024,2048]{1,0:T(8,128)}, u32[]{:S(2)}) copy-start(f32[1024,2048]{1,0:T(8,128)} %get-tuple-element.17) | copy-start | bytes 25165828
